TPU v7x, 32 devices: a whole 2x2x4 slice. The times are simulated.
32 devices in a mesh: sample: 4 (over z), sect: 4 (over x, core), dom: 2 (over y).
Axes of the slice: x: 2, y: 2, z: 4, core: 2. Of those that a mesh axis runs over, the one named last changes fastest.
Arguments:
- features: bfloat16 [8, 512, 512], P(('sample', 'dom'), 'sect'), may hold values from -6 to 6
- weight: bfloat16 [4608, 512], P('sample', 'sect'), may hold values from -0.09375 to 0.09375
- style: float32 [8, 512], P(('sample', 'dom')), may hold values from 0.3 to 3
- bias: float32 [512], P('sect'), may hold values from -3 to 3
- adjoint: bfloat16 [8, 512, 512], P(('sample', 'dom'), 'sect'), may hold values from -6 to 6
Outputs:
- styled: bfloat16 [8, 512, 512], P(('sample', 'dom'), 'sect')
- grad_weight: float32 [4608, 512], P(('sample', 'dom'), 'sect')
- grad_features: bfloat16 [8, 512, 512], P(('sample', 'dom'), 'sect')
All inputs are finite; a program needn't handle non-finite values.
Results may differ from a plain program's by a relative error of at most 0.0049.
Values may be sent and summed in bfloat16 or wider, within the bound.
A program may use at most 64 MiB of HBM per device.

v0:
```python
import jax
import jax.numpy as jnp
from jax import lax
from jax.sharding import PartitionSpec as P

WIDTH = 64
ROWS = 8


OFFSETS = [(-1, -1), (-1, 0), (-1, 1), (0, -1), (0, 0), (0, 1), (1, -1), (1, 0), (1, 1)]
EPSILON = 1e-08


def moved(array, row_step, col_step):
    count = array.shape[0]
    depth = array.shape[1]
    grid = array.reshape(count, depth, ROWS, WIDTH)
    padded = jnp.pad(grid, ((0, 0), (0, 0), (1, 1), (1, 1)))
    part = padded[:, :, 1 + row_step : 1 + row_step + ROWS, 1 + col_step : 1 + col_step + WIDTH]
    return part.reshape(count, depth, ROWS * WIDTH)


def per_device(features, weight, style, bias, adjoint):
    local_ch = features.shape[1]
    sect_count = lax.axis_size("sect")
    sect_place = lax.axis_index("sect")
    channels = local_ch * sect_count
    samples = features.shape[0]
    pixels = features.shape[2]
    own_style = lax.dynamic_slice_in_dim(style, sect_place * local_ch, local_ch, 1)
    local_mod = (features.astype(jnp.float32) * own_style[:, :, None]).astype(jnp.bfloat16)
    modulated = lax.all_gather(local_mod, "sect", axis=1, tiled=True)
    full_weight = lax.all_gather(weight, "sample", axis=0, tiled=True)
    kernel = full_weight.reshape(9, channels, local_ch)
    kernel_f = kernel.astype(jnp.float32)
    shifts = [moved(modulated, row_step, col_step) for row_step, col_step in OFFSETS]
    conv_out = jnp.zeros(features.shape, jnp.float32)
    for index in range(9):
        conv_out = conv_out + jnp.einsum(
            "nip,io->nop", shifts[index], kernel[index], preferred_element_type=jnp.float32
        )
    kernel_sq = jnp.sum(kernel_f * kernel_f, axis=0)
    style_sq = style * style
    energy = jnp.dot(style_sq, kernel_sq, precision=lax.Precision.HIGHEST) + EPSILON
    demod = lax.rsqrt(energy)
    styled = (conv_out * demod[:, :, None] + bias[None, :, None]).astype(jnp.bfloat16)
    adjoint_f = adjoint.astype(jnp.float32)
    scaled_adjoint = (adjoint_f * demod[:, :, None]).astype(jnp.bfloat16)
    demod_grad = jnp.sum(adjoint_f * conv_out, axis=2)
    energy_grad = -0.5 * demod_grad * demod * demod * demod
    coupling = jnp.dot(style_sq.T, energy_grad, precision=lax.Precision.HIGHEST)
    grads = []
    for index in range(9):
        grads.append(
            jnp.einsum(
                "nip,nop->io", shifts[index], scaled_adjoint, preferred_element_type=jnp.float32
            )
            + 2.0 * kernel_f[index] * coupling
        )
    grad_terms = jnp.concatenate(grads, axis=0)
    grad_weight = lax.psum_scatter(grad_terms, ("sample", "dom"), scatter_dimension=0, tiled=True)
    back = jnp.zeros((samples, channels, pixels), jnp.float32)
    for index in range(9):
        row_step, col_step = OFFSETS[index]
        partial_back = jnp.einsum(
            "nop,io->nip", scaled_adjoint, kernel[index], preferred_element_type=jnp.float32
        )
        back = back + moved(partial_back, -row_step, -col_step)
    summed = lax.psum_scatter(back, "sect", scatter_dimension=1, tiled=True)
    grad_features = (summed * own_style[:, :, None]).astype(jnp.bfloat16)
    return (styled, grad_weight, grad_features)


def solution(mesh):
    in_specs = (
        P(("sample", "dom"), "sect", None),
        P("sample", "sect"),
        P(("sample", "dom"), None),
        P("sect"),
        P(("sample", "dom"), "sect", None),
    )
    out_specs = (
        P(("sample", "dom"), "sect", None),
        P(("sample", "dom"), "sect"),
        P(("sample", "dom"), "sect", None),
    )
    return jax.shard_map(
        per_device, mesh=mesh, in_specs=in_specs, out_specs=out_specs, check_vma=False
    )
```

profile of v0, /device:TPU:0, one launch (start us, length us, event | category | flops | bytes accessed | tf_op | source)
XLA Modules:
  0.0 160.6 jit_solution(1903137504310892271)
XLA Ops:
  7.2 0.7 all-gather.2.cloned.1.call-update
  7.9 1.0 copy.8
  9.0 1.7 %copy.9 = bf16[1,128,512]{1,2,0:T(8,128)(2,1)} copy(bf16[1,128,512]{2,1,0:T(8,128)(2,1)} %param.9) | data formatting | bytes 262144 | tf_op args[4]
  10.6 0.8 mul.143
  11.4 0.7 dynamic-slice_bitcast_fusion
  12.1 8.6 %all_gather.6 = bf16[1,512,512]{1,2,0:T(8,128)(2,1)S(1)} all-gather(bf16[1,128,512]{1,2,0:T(8,128)(2,1)S(1)} %multiply_convert_fusion.1), channel_id=1, replica_groups=mesh['sample'=4,'sect'=4,'dom'=2] {'sect'}, dimensions={1}, use_global_device_ids=true | all-gather | bytes 655360 | tf_op jit(solution)/shard_map/all_gather | solution.py:32
  20.7 0.8 copy-done.1
  21.5 2.1 %pad_slice_fusion.8 = (bf16[1,512,8,64]{1,3,2,0:T(8,128)(2,1)}, bf16[1,512,8,64]{1,3,2,0:T(8,128)(2,1)}, bf16[1,512,8,64]{1,3,2,0:T(8,128)(2,1)}, bf16[1,512,8,6...) fusion(bf16[1,512,8,64]{1,3,2,0:T(8,128)(2,1)S(1)} %bitcast.176), kind=kLoop, calls=%fused_computation.64 | loop fusion | bytes 4718592 | tf_op jit(solution)/shard_map/slice | solution.py:19
  23.7 19.1 %all-gather.2.cloned.1.call-done = bf16[4608,128]{1,0:T(8,128)(2,1)} async-done(((bf16[1152,128]{1,0:T(8,128)(2,1)}), bf16[4608,128]{1,0:T(8,128)(2,1)}) %all-gather.2.cloned.1.call-update) | async-done | bytes 1179664 | tf_op jit(solution)/shard_map/all_gather | solution.py:33
  42.7 1.4 convert_multiply_fusion
  44.2 0.8 reduce_sum.18
  45.0 1.3 fusion.16
  46.3 1.4 fusion.62
  50.9 1.0 fusion.23
  54.7 0.5 fusion.19
  55.2 1.4 fusion.5
  56.9 0.8 copy-done.14
  57.8 1.1 fusion.14
  58.8 1.0 fusion.13
  59.9 1.0 fusion.12
  60.9 1.1 fusion.11
  62.0 1.0 fusion.10
  63.0 1.0 fusion.9
  64.1 1.0 fusion.8
  65.1 1.1 fusion.7
  66.2 1.1 fusion.6
  67.2 0.9 copy-done.15
  68.2 0.8 copy.10
  69.0 11.8 %reduce-scatter.5.cloned.1.call-done = f32[1,128,512]{1,2,0:T(8,128)} async-done(((f32[1,512,512]{1,2,0:T(8,128)}), f32[1,128,512]{1,2,0:T(8,128)}) %reduce-scatter.5.cloned.1.call-update) | async-done | bytes 262160 | tf_op jit(solution)/shard_map/reduce_scatter | solution.py:69
  80.8 1.0 multiply_convert_fusion
  81.7 0.8 copy.11
  82.5 71.5 %reduce-scatter.3.cloned.1.call-done = f32[576,128]{1,0:T(8,128)} async-done(((f32[4608,128]{1,0:T(8,128)}), f32[576,128]{1,0:T(8,128)}) %reduce-scatter.3.cloned.1.call-update) | async-done | bytes 294928 | tf_op jit(solution)/shard_map/reduce_scatter | solution.py:61
  (63 shorter events, 6.2 us)
Async XLA Ops:
  7.2 35.6 %all-gather.2.cloned.1.call-start = ((), (), s32[]{:S(2)}) async-start(), calls=%async_computation.2 | async-start | bytes 1474560 | tf_op jit(solution)/shard_map/all_gather | solution.py:33
  7.9 72.9 %reduce-scatter.5.cloned.1.call-start = ((), (), s32[]{:S(2)}) async-start(), calls=%async_computation.4 | async-start | bytes 1310720 | tf_op jit(solution)/shard_map/reduce_scatter | solution.py:69
  20.7 0.8 copy-start.1
  44.2 0.9 copy-start.17
  44.2 2.1 %copy-start = (bf16[4608,128]{1,0:T(8,128)(2,1)S(1)}, bf16[4608,128]{1,0:T(8,128)(2,1)}, u32[]{:S(2)}) copy-start(bf16[4608,128]{1,0:T(8,128)(2,1)} %all-gather.2.cloned.1.call-done) | copy-start | bytes 3538948
  45.0 2.7 %copy-start.12 = (bf16[1,512,8,64]{1,3,2,0:T(8,128)(2,1)S(1)}, bf16[1,512,8,64]{1,3,2,0:T(8,128)(2,1)}, u32[]{:S(2)}) copy-start(bf16[1,512,8,64]{1,3,2,0:T(8,128)(2,1)} %get-tuple-element.7) | copy-start | bytes 1572868
  45.0 3.0 %copy-start.10 = (bf16[1,512,8,64]{1,3,2,0:T(8,128)(2,1)S(1)}, bf16[1,512,8,64]{1,3,2,0:T(8,128)(2,1)}, u32[]{:S(2)}) copy-start(bf16[1,512,8,64]{1,3,2,0:T(8,128)(2,1)} %get-tuple-element.8) | copy-start | bytes 1572868
  46.3 2.0 %copy-start.8 = (bf16[1,512,8,64]{1,3,2,0:T(8,128)(2,1)S(1)}, bf16[1,512,8,64]{1,3,2,0:T(8,128)(2,1)}, u32[]{:S(2)}) copy-start(bf16[1,512,8,64]{1,3,2,0:T(8,128)(2,1)} %get-tuple-element.9) | copy-start | bytes 1572868
  48.0 1.0 copy-start.2
  48.4 1.1 copy-start.6
  49.1 1.1 copy-start.5
  49.4 1.1 copy-start.4
  49.7 1.1 copy-start.3
  49.7 1.1 copy-start.16
  56.7 97.4 %reduce-scatter.3.cloned.1.call-start = ((), (), s32[]{:S(2)}) async-start(), calls=%async_computation.3 | async-start | bytes 2654208 | tf_op jit(solution)/shard_map/reduce_scatter | solution.py:61
  56.7 1.0 copy-start.14
  56.7 2.1 %copy-start.13 = (bf16[1,512,8,64]{1,3,2,0:T(8,128)(2,1)S(1)}, bf16[1,512,8,64]{1,3,2,0:T(8,128)(2,1)}, u32[]{:S(2)}) copy-start(bf16[1,512,8,64]{1,3,2,0:T(8,128)(2,1)} %get-tuple-element.7) | copy-start | bytes 1572868
  56.9 3.0 %copy-start.11 = (bf16[1,512,8,64]{1,3,2,0:T(8,128)(2,1)S(1)}, bf16[1,512,8,64]{1,3,2,0:T(8,128)(2,1)}, u32[]{:S(2)}) copy-start(bf16[1,512,8,64]{1,3,2,0:T(8,128)(2,1)} %get-tuple-element.8) | copy-start | bytes 1572868
  58.8 2.1 %copy-start.9 = (bf16[1,512,8,64]{1,3,2,0:T(8,128)(2,1)S(1)}, bf16[1,512,8,64]{1,3,2,0:T(8,128)(2,1)}, u32[]{:S(2)}) copy-start(bf16[1,512,8,64]{1,3,2,0:T(8,128)(2,1)} %get-tuple-element.9) | copy-start | bytes 1572868
  60.9 2.1 %copy-start.7 = (bf16[1,512,8,64]{1,3,2,0:T(8,128)(2,1)S(1)}, bf16[1,512,8,64]{1,3,2,0:T(8,128)(2,1)}, u32[]{:S(2)}) copy-start(bf16[1,512,8,64]{1,3,2,0:T(8,128)(2,1)} %get-tuple-element.10) | copy-start | bytes 1572868
  67.2 0.9 copy-start.15
  67.2 1.0 copy-start.18
Sparse Core Ops, SparseCore 0:
  9.6 33.1 all-gather.1
  56.8 23.9 reduce-scatter.4
  85.3 68.7 reduce-scatter.2
where the time goes:
time: 161 us
  waiting for transfers between devices  103 us (64%)
  matrix products  18.9 us (12%)
  between operations  14 us (9%)
  local copies, waits for them, and re-layouts  11.1 us (7%)
  blocking collectives  8.62 us (5%)
  other arithmetic  4.68 us (3%)
    reduce_scatter x1, waiting for transfers between devices, per_device(): lax.psum_scatter(grad_terms, ('sample', 'dom'), scatter_dimension=0, tile...  71.5 us
    all_gather x1, waiting for transfers between devices, per_device(): full_weight = lax.all_gather(weight, 'sample', axis=0, tiled=True)  19.1 us
    reduce_scatter x1, waiting for transfers between devices, per_device(): summed = lax.psum_scatter(back, 'sect', scatter_dimension=1, tiled=True)  11.8 us
    dot_general x9, matrix products, per_device(): jnp.einsum('nip,nop->io', shifts[index], scaled_adjoint, preferred_elemen...  9.43 us
    all_gather x1, blocking collectives, per_device(): modulated = lax.all_gather(local_mod, 'sect', axis=1, tiled=True)  8.62 us
    unnamed x42, local copies, waits for them, and re-layouts  7.83 us
    dot_general x9, matrix products, per_device(): jnp.einsum('nip,io->nop', shifts[index], kernel[index], preferred_element...  4.48 us
    dot_general x9, matrix products, per_device(): jnp.einsum('nop,io->nip', scaled_adjoint, kernel[index], preferred_elemen...  3.75 us
  transfers between devices with their start and end apart: 3, of which 3 were waited for; matrix products, arithmetic and copies ran while one was open for 11% of the time, Pallas kernels for 0%

commit v1 on v0

--- a/solution.py
+++ b/solution.py
@@ -1,6 +1,8 @@
 import jax
 import jax.numpy as jnp
 from jax import lax
+from jax.experimental import pallas as pl
+from jax.experimental.pallas import tpu as pltpu
 from jax.sharding import PartitionSpec as P
 
 WIDTH = 64
@@ -71,6 +73,288 @@
     return (styled, grad_weight, grad_features)
 
 
+MESH = pl.DeviceIdType.MESH
+HIGH = lax.Precision.HIGHEST
+F32 = jnp.float32
+BF16 = jnp.bfloat16
+CH = 512
+BLOCK = 128
+PIXELS = ROWS * WIDTH
+OWN = 1152
+HALF = 576
+
+
+def fits(mesh):
+    return mesh.shape["sample"] == 4 and mesh.shape["sect"] == 4 and mesh.shape["dom"] == 2
+
+
+def shifted_by(array, row_step, col_step):
+    step = row_step * WIDTH + col_step
+    if step == 0:
+        return array
+    place = lax.broadcasted_iota(jnp.int32, (1, PIXELS), 1)
+    col = jnp.bitwise_and(place, WIDTH - 1) + col_step
+    full = place + row_step * WIDTH
+    ok = (col >= 0) & (col < WIDTH) & (full >= 0) & (full < PIXELS)
+    rolled = pltpu.roll(array, (-step) % PIXELS, 1)
+    return jnp.where(ok, rolled, 0.0)
+
+
+def column(row):
+    return jnp.transpose(jnp.broadcast_to(row, (BLOCK, BLOCK)))[:, 0:1]
+
+
+def as_row(col):
+    return jnp.transpose(jnp.broadcast_to(col, (BLOCK, BLOCK)))[0:1, :]
+
+
+def fused_kernel(
+    features, weight, style, bias, adjoint, styled, grad_weight, grad_features,
+    kern, mod, adj, grad, grad_b, from_dom, to_sample, from_sample, to_sect, from_sect,
+    twice, style_all, energy_out, energy_in, egrad_all,
+    style_s, style_r, mod_s, mod_r, w_s, w_r, w2_s, w2_r, en_s, en_r,
+    gy_s, gy_r, gz_s, gz_r, bk_s, bk_r, eg_s, eg_r, swap_s, swap_r,
+):
+    s = lax.axis_index("sample")
+    c = lax.axis_index("sect")
+    d = lax.axis_index("dom")
+    other = 1 - d
+
+    def at_sample(k):
+        return {"sample": lax.rem(s + k, 4)}
+
+    def at_sect(k):
+        return {"sect": lax.rem(c + k, 4)}
+
+    partner = {"dom": other}
+
+    def remote(src, dst, send, recv, where):
+        return pltpu.make_async_remote_copy(
+            src_ref=src, dst_ref=dst, send_sem=send, recv_sem=recv, device_id=where, device_id_type=MESH
+        )
+
+    barrier = pltpu.get_barrier_semaphore()
+    for k in (1, 2, 3):
+        pl.semaphore_signal(barrier, inc=1, device_id=at_sample(k), device_id_type=MESH)
+        pl.semaphore_signal(barrier, inc=1, device_id=at_sect(k), device_id_type=MESH)
+    pl.semaphore_signal(barrier, inc=1, device_id=partner, device_id_type=MESH)
+
+    own_channels = pl.ds(pl.multiple_of(c * BLOCK, BLOCK), BLOCK)
+    style_col = column(style[:, own_channels])
+    mod[own_channels, :] = (features[0].astype(F32) * style_col).astype(BF16)
+    style_all[0, 0] = style[...]
+    own_rows = pl.ds(pl.multiple_of(s * OWN, OWN), OWN)
+    kern[own_rows, :] = weight[...]
+
+    def rows_of(shard, part):
+        return pl.ds(pl.multiple_of(shard * OWN + part * HALF, HALF), HALF)
+
+    pl.semaphore_wait(barrier, 7)
+
+    style_c = [
+        remote(style_all.at[0, 0], style_all.at[0, k], style_s.at[k], style_r.at[k], at_sample(k)) for k in (1, 2, 3)
+    ]
+    for copy in style_c:
+        copy.start()
+    mod_c = [
+        remote(mod.at[own_channels], mod.at[own_channels], mod_s.at[k], mod_r.at[k], at_sect(k)) for k in (1, 2, 3)
+    ]
+    for copy in mod_c:
+        copy.start()
+    w_c = [
+        remote(
+            weight.at[pl.ds(pl.multiple_of(d * HALF, HALF), HALF)],
+            kern.at[rows_of(s, d)],
+            w_s.at[k],
+            w_r.at[k],
+            at_sample(k),
+        )
+        for k in (1, 2, 3)
+    ]
+    for k in (2, 1, 3):
+        w_c[k - 1].start()
+
+    squares = weight[...].astype(F32)
+    squares = squares * squares
+    part = squares[0:CH] + squares[CH : 2 * CH]
+    tail = part[0:BLOCK] + squares[2 * CH : OWN]
+    twice[0:BLOCK] = tail
+    twice[BLOCK:CH] = part[BLOCK:]
+    twice[CH : CH + BLOCK] = tail
+    twice[CH + BLOCK : 2 * CH] = part[BLOCK:]
+    kernel_sq = twice[pl.ds(pl.multiple_of(CH - s * BLOCK, BLOCK), CH), :]
+    for copy in style_c:
+        copy.wait_recv()
+    swap_style = remote(style_all.at[0], style_all.at[1], swap_s.at[0], swap_r.at[0], partner)
+    swap_style.start()
+    styles = jnp.concatenate([style_all[0, k] for k in range(4)] * 2, axis=0)
+    terms = jnp.dot(styles * styles, kernel_sq, precision=HIGH, preferred_element_type=F32)
+    for k in range(4):
+        energy_out[k] = terms[k : k + 1, :]
+    en_c = [
+        remote(energy_out.at[k], energy_in.at[k], en_s.at[k], en_r.at[k], at_sample(4 - k)) for k in (1, 2, 3)
+    ]
+    for copy in en_c:
+        copy.start()
+    energy = energy_out[0] + EPSILON
+    for k in (1, 2, 3):
+        en_c[k - 1].wait_recv()
+        energy = energy + energy_in[k]
+    demod = column(lax.rsqrt(energy))
+
+    adjoint_f = adjoint[0].astype(F32)
+    scaled = (adjoint_f * demod).astype(BF16).astype(F32)
+    for index in range(9):
+        row_step, col_step = OFFSETS[index]
+        adj[index * BLOCK : (index + 1) * BLOCK, :] = shifted_by(scaled, -row_step, -col_step).astype(BF16)
+    for copy in mod_c:
+        copy.wait_recv()
+
+    for index in range(9):
+        value = lax.dot_general(
+            mod[...],
+            adj[index * BLOCK : (index + 1) * BLOCK, :],
+            (((1,), (1,)), ((), ())),
+            preferred_element_type=F32,
+        )
+        grad[index * CH : (index + 1) * CH, :] = value
+        grad_b[index * CH : (index + 1) * CH, :] = value.astype(BF16)
+    gy_c = [
+        remote(
+            grad_b.at[rows_of(lax.rem(s + k, 4), other)], from_dom.at[k], gy_s.at[k], gy_r.at[k], partner
+        )
+        for k in range(4)
+    ]
+    order = (2, 1, 3, 0)
+    for k in order:
+        gy_c[k].start()
+
+    w2_c = []
+    for k in (1, 3, 2):
+        shard = lax.rem(s + 4 - k, 4)
+        w_c[k - 1].wait_recv()
+        copy = remote(kern.at[rows_of(shard, d)], kern.at[rows_of(shard, d)], w2_s.at[k], w2_r.at[k], partner)
+        copy.start()
+        w2_c.append(copy)
+
+    gz_c = []
+    for k in (2, 1, 3):
+        gy_c[k].wait_recv()
+        kept = grad[rows_of(lax.rem(s + k, 4), d), :]
+        to_sample[k] = (kept + from_dom[k].astype(F32)).astype(BF16)
+        copy = remote(to_sample.at[k], from_sample.at[k], gz_s.at[k], gz_r.at[k], at_sample(k))
+        copy.start()
+        gz_c.append(copy)
+
+    for copy in w2_c:
+        copy.wait_recv()
+
+    wide = adj[...]
+
+    def back_of(block):
+        rows = [
+            kern[pl.ds(pl.multiple_of(index * CH + block * BLOCK, BLOCK), BLOCK), :] for index in range(9)
+        ]
+        return jnp.dot(jnp.concatenate(rows, axis=1), wide, preferred_element_type=F32)
+
+    bk_c = []
+    for k in (2, 1, 3):
+        to_sect[k] = back_of(lax.rem(c + k, 4)).astype(BF16)
+        copy = remote(to_sect.at[k], from_sect.at[k], bk_s.at[k], bk_r.at[k], at_sect(k))
+        copy.start()
+        bk_c.append(copy)
+
+    conv_out = jnp.zeros((BLOCK, PIXELS), F32)
+    for index in range(9):
+        row_step, col_step = OFFSETS[index]
+        value = lax.dot_general(
+            kern[index * CH : (index + 1) * CH, :],
+            mod[...],
+            (((0,), (0,)), ((), ())),
+            preferred_element_type=F32,
+        )
+        conv_out = conv_out + shifted_by(value, row_step, col_step)
+    demod_grad = jnp.sum(adjoint_f * conv_out, axis=1, keepdims=True)
+    egrad_all[0, 0] = as_row(-0.5 * demod_grad * demod * demod * demod)
+    eg_c = [
+        remote(egrad_all.at[0, 0], egrad_all.at[0, k], eg_s.at[k], eg_r.at[k], at_sample(k)) for k in (1, 2, 3)
+    ]
+    for copy in eg_c:
+        copy.start()
+    styled[0] = (conv_out * demod + column(bias[...])).astype(BF16)
+    own_back = back_of(c)
+    for copy in eg_c:
+        copy.wait_recv()
+    swap_egrad = remote(egrad_all.at[0], egrad_all.at[1], swap_s.at[1], swap_r.at[1], partner)
+    swap_egrad.start()
+
+    gy_c[0].wait_recv()
+    total = grad[rows_of(s, d), :] + from_dom[0].astype(F32)
+    for k, copy in zip((2, 1, 3), gz_c):
+        copy.wait_recv()
+        total = total + from_sample[k].astype(F32)
+
+    swap_style.wait_recv()
+    swap_egrad.wait_recv()
+    styles = jnp.concatenate([style_all[h, k] for h in range(2) for k in range(4)], axis=0)
+    egrads = jnp.concatenate([egrad_all[h, k] for h in range(2) for k in range(4)], axis=0)
+    coupling = lax.dot_general(
+        styles * styles, egrads, (((0,), (0,)), ((), ())), precision=HIGH, preferred_element_type=F32
+    )
+    twice[0:CH] = coupling
+    twice[CH : 2 * CH] = coupling
+    first = pl.multiple_of((2 * s + d) * (HALF - CH), HALF - CH)
+    owned = weight[pl.ds(pl.multiple_of(d * HALF, HALF), HALF), :].astype(F32)
+    grad_weight[...] = total + 2.0 * owned * twice[pl.ds(first, HALF), :]
+
+    summed = own_back
+    for k, copy in zip((2, 1, 3), bk_c):
+        copy.wait_recv()
+        summed = summed + from_sect[k].astype(F32)
+    grad_features[0] = (summed * style_col).astype(BF16)
+
+    for copy in style_c + mod_c + w_c + w2_c + en_c + gy_c + gz_c + bk_c + eg_c + [swap_style, swap_egrad]:
+        copy.wait_send()
+
+
+def fused(features, weight, style, bias, adjoint):
+    vmem = pl.BlockSpec(memory_space=pltpu.VMEM)
+    dma = pltpu.SemaphoreType.DMA((4,))
+    return tuple(
+        pl.pallas_call(
+            fused_kernel,
+            out_shape=(
+                jax.ShapeDtypeStruct(features.shape, BF16),
+                jax.ShapeDtypeStruct((HALF, BLOCK), F32),
+                jax.ShapeDtypeStruct(features.shape, BF16),
+            ),
+            in_specs=[vmem] * 5,
+            out_specs=(vmem,) * 3,
+            scratch_shapes=[
+                pltpu.VMEM((9 * CH, BLOCK), BF16),
+                pltpu.VMEM((CH, PIXELS), BF16),
+                pltpu.VMEM((9 * BLOCK, PIXELS), BF16),
+                pltpu.VMEM((9 * CH, BLOCK), F32),
+                pltpu.VMEM((9 * CH, BLOCK), BF16),
+                pltpu.VMEM((4, HALF, BLOCK), BF16),
+                pltpu.VMEM((4, HALF, BLOCK), BF16),
+                pltpu.VMEM((4, HALF, BLOCK), BF16),
+                pltpu.VMEM((4, BLOCK, PIXELS), BF16),
+                pltpu.VMEM((4, BLOCK, PIXELS), BF16),
+                pltpu.VMEM((2 * CH, BLOCK), F32),
+                pltpu.VMEM((2, 4, 1, CH), F32),
+                pltpu.VMEM((4, 1, BLOCK), F32),
+                pltpu.VMEM((4, 1, BLOCK), F32),
+                pltpu.VMEM((2, 4, 1, BLOCK), F32),
+            ]
+            + [dma] * 20,
+            compiler_params=pltpu.CompilerParams(
+                collective_id=0, has_side_effects=True, vmem_limit_bytes=40 * 1024 * 1024
+            ),
+        )(features, weight, style, bias.reshape(1, BLOCK), adjoint)
+    )
+
+
 def solution(mesh):
     in_specs = (
         P(("sample", "dom"), "sect", None),
@@ -84,6 +368,7 @@
         P(("sample", "dom"), "sect"),
         P(("sample", "dom"), "sect", None),
     )
+    body = fused if fits(mesh) else per_device
     return jax.shard_map(
-        per_device, mesh=mesh, in_specs=in_specs, out_specs=out_specs, check_vma=False
-    )
+        body, mesh=mesh, in_specs=in_specs, out_specs=out_specs, check_vma=False
+    )

time: 161 us -> 61.3 us (0.38)
  waiting for transfers between devices: 103 us -> 0 us
  Pallas kernels: 0 us -> 54.3 us
  matrix products: 18.9 us -> 0 us
  between operations: 14 us -> 0.65 us
  blocking collectives: 8.62 us -> 0 us
  local copies, waits for them, and re-layouts: 11.1 us -> 6.12 us
  other arithmetic: 4.68 us -> 0 us
    reduce_scatter x2 -> x0, waiting for transfers between devices: 83.4 us -> none  [the longest x1 71.5 us: per_device(): lax.psum_scatter(grad_terms, ('sample', 'dom'), scatter_dimension=0, tile...]
    pallas_call x0 -> x1, Pallas kernels: none -> 54.3 us  [fused(): pl.pallas_call(fused_kernel, out_shape=(jax.ShapeDtypeStruct(features.sha...]
    all_gather x1 -> x0, waiting for transfers between devices: 19.1 us -> none  [per_device(): full_weight = lax.all_gather(weight, 'sample', axis=0, tiled=True)]
    dot_general x28 -> x0, matrix products: 18.9 us -> none  [the longest x9 9.43 us: per_device(): jnp.einsum('nip,nop->io', shifts[index], scaled_adjoint, preferred_elemen...]
    all_gather x1 -> x0, blocking collectives: 8.62 us -> none  [per_device(): modulated = lax.all_gather(local_mod, 'sect', axis=1, tiled=True)]
    slice x5 -> x0, local copies, waits for them, and re-layouts: 2.58 us -> none  [moved(): padded[:, :, 1 + row_step:1 + row_step + ROWS, 1 + col_step:1 + col_step...]
    mul x3 -> x0, other arithmetic: 2.19 us -> none  [the longest x1 1.42 us: per_device(): kernel_sq = jnp.sum(kernel_f * kernel_f, axis=0)]
    unnamed x42 -> x13, local copies, waits for them, and re-layouts: 7.83 us -> 6.12 us
  transfers between devices with their start and end apart: 3 -> 0, of which waited for: 3 -> 0; matrix products, arithmetic and copies ran while one was open for 11% -> 0% of each run, Pallas kernels for 0% -> 0%
where the time goes in v1:
time: 61.3 us; the launch traced here: 61.1 us
  Pallas kernels  54.3 us (89%)
  local copies, waits for them, and re-layouts  6.12 us (10%)
  between operations  0.65 us (1%)
    pallas_call x1, Pallas kernels, fused(): pl.pallas_call(fused_kernel, out_shape=(jax.ShapeDtypeStruct(features.sha...  54.3 us
    unnamed x13, local copies, waits for them, and re-layouts  6.12 us

profile of v1, /device:TPU:0, one launch (start us, length us, event | category | flops | bytes accessed | tf_op | source)
XLA Modules:
  0.0 61.1 jit_solution(8251752038972166185)
XLA Ops:
  0.6 0.0 copy-start.4
  0.6 0.6 %copy-done.4 = f32[128]{0:T(128)S(1)} copy-done((f32[128]{0:T(128)S(1)}, f32[128]{0:T(128)}, u32[]{:S(2)}) %copy-start.4) | copy-done | bytes 536
  1.3 0.0 copy-start
  1.3 1.0 %copy-done = bf16[1152,128]{1,0:T(8,128)(2,1)S(1)} copy-done((bf16[1152,128]{1,0:T(8,128)(2,1)S(1)}, bf16[1152,128]{1,0:T(8,128)(2,1)}, u32[]{:S(2)}) %copy-start) | copy-done | bytes 294936
  2.2 0.0 copy-start.1
  2.3 0.9 %copy-done.1 = bf16[1,128,512]{2,1,0:T(8,128)(2,1)S(1)} copy-done((bf16[1,128,512]{2,1,0:T(8,128)(2,1)S(1)}, bf16[1,128,512]{2,1,0:T(8,128)(2,1)}, u32[]{:S(2)}) %copy-start.1) | copy-done | bytes 131096
  3.2 0.0 copy-start.2
  3.2 0.9 %copy-done.2 = bf16[1,128,512]{2,1,0:T(8,128)(2,1)S(1)} copy-done((bf16[1,128,512]{2,1,0:T(8,128)(2,1)S(1)}, bf16[1,128,512]{2,1,0:T(8,128)(2,1)}, u32[]{:S(2)}) %copy-start.2) | copy-done | bytes 131096
  4.1 0.0 copy-start.3
  4.1 0.7 %copy-done.3 = f32[1,512]{1,0:T(1,128)S(1)} copy-done((f32[1,512]{1,0:T(1,128)S(1)}, f32[1,512]{1,0:T(1,128)}, u32[]{:S(2)}) %copy-start.3) | copy-done | bytes 2072
  4.7 54.3 %shard_map.76 = (bf16[1,128,512]{2,1,0:T(8,128)(2,1)S(1)}, f32[576,128]{1,0:T(8,128)S(1)}, bf16[1,128,512]{2,1,0:T(8,128)(2,1)S(1)}) custom-call(bf16[1,128,512]{2,1,0:T(8,128)(2,1)S(1)} %copy-done.1, bf16[1152,128]{1,0:T(8,128)(2,1)S(1)} %copy-done, f32[1,512]{1,0:T(1,128)S(1)} %copy-done.3, f32[1,128]{1,0:T(1,128)S(1)} %bitcast.1, ...), custom_call_target="tpu_custom_call" | custom-call | tf_op jit(solution)/shard_map/pallas_call | solution.py:324
  59.1 0.7 %copy.11 = bf16[1,128,512]{2,1,0:T(8,128)(2,1)} copy(bf16[1,128,512]{2,1,0:T(8,128)(2,1)S(1)} %get-tuple-element.6) | data formatting | bytes 262144
  59.8 0.7 %copy.12 = f32[576,128]{1,0:T(8,128)} copy(f32[576,128]{1,0:T(8,128)S(1)} %get-tuple-element.7) | data formatting | bytes 589824
  60.5 0.7 %copy.13 = bf16[1,128,512]{2,1,0:T(8,128)(2,1)} copy(bf16[1,128,512]{2,1,0:T(8,128)(2,1)S(1)} %get-tuple-element.8) | data formatting | bytes 262144
Async XLA Ops:
  0.6 0.7 %copy-start.4 = (f32[128]{0:T(128)S(1)}, f32[128]{0:T(128)}, u32[]{:S(2)}) copy-start(f32[128]{0:T(128)} %param.8) | copy-start | bytes 1540
  1.3 1.0 %copy-start = (bf16[1152,128]{1,0:T(8,128)(2,1)S(1)}, bf16[1152,128]{1,0:T(8,128)(2,1)}, u32[]{:S(2)}) copy-start(bf16[1152,128]{1,0:T(8,128)(2,1)} %weight.1) | copy-start | bytes 884740
  2.2 0.9 %copy-start.1 = (bf16[1,128,512]{2,1,0:T(8,128)(2,1)S(1)}, bf16[1,128,512]{2,1,0:T(8,128)(2,1)}, u32[]{:S(2)}) copy-start(bf16[1,128,512]{2,1,0:T(8,128)(2,1)} %features.1) | copy-start | bytes 393220
  3.2 0.9 %copy-start.2 = (bf16[1,128,512]{2,1,0:T(8,128)(2,1)S(1)}, bf16[1,128,512]{2,1,0:T(8,128)(2,1)}, u32[]{:S(2)}) copy-start(bf16[1,128,512]{2,1,0:T(8,128)(2,1)} %adjoint.1) | copy-start | bytes 393220
  4.1 0.7 %copy-start.3 = (f32[1,512]{1,0:T(1,128)S(1)}, f32[1,512]{1,0:T(1,128)}, u32[]{:S(2)}) copy-start(f32[1,512]{1,0:T(1,128)} %style.1) | copy-start | bytes 6148

commit v2 on v1

--- a/solution.py
+++ b/solution.py
@@ -88,16 +88,17 @@
     return mesh.shape["sample"] == 4 and mesh.shape["sect"] == 4 and mesh.shape["dom"] == 2
 
 
-def shifted_by(array, row_step, col_step):
-    step = row_step * WIDTH + col_step
-    if step == 0:
-        return array
-    place = lax.broadcasted_iota(jnp.int32, (1, PIXELS), 1)
-    col = jnp.bitwise_and(place, WIDTH - 1) + col_step
-    full = place + row_step * WIDTH
-    ok = (col >= 0) & (col < WIDTH) & (full >= 0) & (full < PIXELS)
-    rolled = pltpu.roll(array, (-step) % PIXELS, 1)
-    return jnp.where(ok, rolled, 0.0)
+def moved_rows(array, row_step, col_step):
+    if col_step != 0:
+        place = lax.broadcasted_iota(jnp.int32, (PIXELS, 1), 0)
+        col = jnp.bitwise_and(place, WIDTH - 1) + col_step
+        array = jnp.where((col >= 0) & (col < WIDTH), pltpu.roll(array, (-col_step) % PIXELS, 0), 0.0)
+    edge = jnp.zeros((WIDTH, array.shape[1]), array.dtype)
+    if row_step == 1:
+        array = jnp.concatenate([array[WIDTH:], edge], axis=0)
+    if row_step == -1:
+        array = jnp.concatenate([edge, array[:-WIDTH]], axis=0)
+    return array
 
 
 def column(row):
@@ -109,8 +110,8 @@
 
 
 def fused_kernel(
-    features, weight, style, bias, adjoint, styled, grad_weight, grad_features,
-    kern, mod, adj, grad, grad_b, from_dom, to_sample, from_sample, to_sect, from_sect,
+    features_h, weight_h, style_h, bias_h, adjoint_h, styled, grad_weight, grad_features,
+    features, bias, adjoint, in_s, kern, mod, mod_t, adj, grad, grad_b, from_dom, to_sample, from_sample, to_sect, from_sect,
     twice, style_all, energy_out, energy_in, egrad_all,
     style_s, style_r, mod_s, mod_r, w_s, w_r, w2_s, w2_r, en_s, en_r,
     gy_s, gy_r, gz_s, gz_r, bk_s, bk_r, eg_s, eg_r, swap_s, swap_r,
@@ -133,6 +134,23 @@
             src_ref=src, dst_ref=dst, send_sem=send, recv_sem=recv, device_id=where, device_id_type=MESH
         )
 
+    style_all_own = style_all.at[0, 0]
+    own_rows = pl.ds(pl.multiple_of(s * OWN, OWN), OWN)
+    loads = [
+        pltpu.make_async_copy(source, target, in_s.at[index])
+        for index, (source, target) in enumerate(
+            (
+                (style_h, style_all_own),
+                (features_h.at[0], features),
+                (weight_h, kern.at[own_rows]),
+                (adjoint_h.at[0], adjoint),
+                (bias_h, bias),
+            )
+        )
+    ]
+    for load in loads:
+        load.start()
+
     barrier = pltpu.get_barrier_semaphore()
     for k in (1, 2, 3):
         pl.semaphore_signal(barrier, inc=1, device_id=at_sample(k), device_id_type=MESH)
@@ -140,41 +158,45 @@
     pl.semaphore_signal(barrier, inc=1, device_id=partner, device_id_type=MESH)
 
     own_channels = pl.ds(pl.multiple_of(c * BLOCK, BLOCK), BLOCK)
-    style_col = column(style[:, own_channels])
-    mod[own_channels, :] = (features[0].astype(F32) * style_col).astype(BF16)
-    style_all[0, 0] = style[...]
-    own_rows = pl.ds(pl.multiple_of(s * OWN, OWN), OWN)
-    kern[own_rows, :] = weight[...]
+    for load in loads[0:3]:
+        load.wait()
+    style_col = column(style_all[0, 0, :, own_channels])
+    mod[own_channels, :] = (features[...].astype(F32) * style_col).astype(BF16)
 
     def rows_of(shard, part):
         return pl.ds(pl.multiple_of(shard * OWN + part * HALF, HALF), HALF)
 
-    pl.semaphore_wait(barrier, 7)
-
-    style_c = [
-        remote(style_all.at[0, 0], style_all.at[0, k], style_s.at[k], style_r.at[k], at_sample(k)) for k in (1, 2, 3)
-    ]
-    for copy in style_c:
-        copy.start()
-    mod_c = [
-        remote(mod.at[own_channels], mod.at[own_channels], mod_s.at[k], mod_r.at[k], at_sect(k)) for k in (1, 2, 3)
-    ]
-    for copy in mod_c:
-        copy.start()
-    w_c = [
-        remote(
-            weight.at[pl.ds(pl.multiple_of(d * HALF, HALF), HALF)],
-            kern.at[rows_of(s, d)],
-            w_s.at[k],
-            w_r.at[k],
-            at_sample(k),
-        )
-        for k in (1, 2, 3)
-    ]
-    for k in (2, 1, 3):
-        w_c[k - 1].start()
-
-    squares = weight[...].astype(F32)
+    def along(up, j):
+        half = kern.at[rows_of(s - j if up else s + j, d)]
+        slot = j if up else 3 + j
+        return remote(half, half, w_s.at[slot], w_r.at[slot], at_sample(1 if up else 3))
+
+    def across(up, j):
+        half = kern.at[rows_of(s - 1 - j if up else s + 1 + j, d)]
+        slot = j if up else 3 + j
+        return remote(half, half, w2_s.at[slot], w2_r.at[slot], partner)
+
+    def sends(up, j):
+        return (s >= j) & (s < 3) if up else (s <= 3 - j) & (s > 0)
+
+    def gets(up, j):
+        return s >= j + 1 if up else s <= 2 - j
+
+    def pass_on(j):
+        for up in (True, False):
+
+            @pl.when(gets(up, j))
+            def _():
+                along(up, j).wait_recv()
+                across(up, j).start()
+
+            if j < 2:
+
+                @pl.when(sends(up, j + 1))
+                def _():
+                    along(up, j + 1).start()
+
+    squares = kern[own_rows, :].astype(F32)
     squares = squares * squares
     part = squares[0:CH] + squares[CH : 2 * CH]
     tail = part[0:BLOCK] + squares[2 * CH : OWN]
@@ -183,6 +205,25 @@
     twice[CH : CH + BLOCK] = tail
     twice[CH + BLOCK : 2 * CH] = part[BLOCK:]
     kernel_sq = twice[pl.ds(pl.multiple_of(CH - s * BLOCK, BLOCK), CH), :]
+
+    pl.semaphore_wait(barrier, 7)
+
+    style_c = [
+        remote(style_all.at[0, 0], style_all.at[0, k], style_s.at[k], style_r.at[k], at_sample(k)) for k in (1, 2, 3)
+    ]
+    for copy in style_c:
+        copy.start()
+    for up in (True, False):
+
+        @pl.when(sends(up, 0))
+        def _():
+            along(up, 0).start()
+
+    mod_c = [
+        remote(mod.at[own_channels], mod.at[own_channels], mod_s.at[k], mod_r.at[k], at_sect(k)) for k in (1, 2, 3)
+    ]
+    for copy in mod_c:
+        copy.start()
     for copy in style_c:
         copy.wait_recv()
     swap_style = remote(style_all.at[0], style_all.at[1], swap_s.at[0], swap_r.at[0], partner)
@@ -196,29 +237,34 @@
     ]
     for copy in en_c:
         copy.start()
+    pass_on(0)
     energy = energy_out[0] + EPSILON
     for k in (1, 2, 3):
         en_c[k - 1].wait_recv()
         energy = energy + energy_in[k]
     demod = column(lax.rsqrt(energy))
 
-    adjoint_f = adjoint[0].astype(F32)
+    loads[3].wait()
+    loads[4].wait()
+    adjoint_f = adjoint[...].astype(F32)
     scaled = (adjoint_f * demod).astype(BF16).astype(F32)
-    for index in range(9):
-        row_step, col_step = OFFSETS[index]
-        adj[index * BLOCK : (index + 1) * BLOCK, :] = shifted_by(scaled, -row_step, -col_step).astype(BF16)
+    scaled_t = jnp.transpose(scaled)
+    for col_step in (-1, 0, 1):
+        by_col = moved_rows(scaled_t, 0, -col_step)
+        for row_step in (-1, 0, 1):
+            index = OFFSETS.index((row_step, col_step))
+            adj[:, index * BLOCK : (index + 1) * BLOCK] = moved_rows(by_col, -row_step, 0).astype(BF16)
     for copy in mod_c:
         copy.wait_recv()
-
-    for index in range(9):
-        value = lax.dot_general(
-            mod[...],
-            adj[index * BLOCK : (index + 1) * BLOCK, :],
-            (((1,), (1,)), ((), ())),
-            preferred_element_type=F32,
-        )
-        grad[index * CH : (index + 1) * CH, :] = value
-        grad_b[index * CH : (index + 1) * CH, :] = value.astype(BF16)
+    pass_on(1)
+
+    for index in range(0, 9, 2):
+        last = min(index + 2, 9)
+        value = jnp.dot(mod[...], adj[:, index * BLOCK : last * BLOCK], preferred_element_type=F32)
+        for one in range(index, last):
+            block = value[:, (one - index) * BLOCK : (one - index + 1) * BLOCK]
+            grad[one * CH : (one + 1) * CH, :] = block
+            grad_b[one * CH : (one + 1) * CH, :] = block.astype(BF16)
     gy_c = [
         remote(
             grad_b.at[rows_of(lax.rem(s + k, 4), other)], from_dom.at[k], gy_s.at[k], gy_r.at[k], partner
@@ -229,14 +275,52 @@
     for k in order:
         gy_c[k].start()
 
-    w2_c = []
-    for k in (1, 3, 2):
-        shard = lax.rem(s + 4 - k, 4)
-        w_c[k - 1].wait_recv()
-        copy = remote(kern.at[rows_of(shard, d)], kern.at[rows_of(shard, d)], w2_s.at[k], w2_r.at[k], partner)
-        copy.start()
-        w2_c.append(copy)
-
+    pass_on(2)
+    mod_t[...] = jnp.transpose(mod[...])
+    for j in range(3):
+        for up in (True, False):
+
+            @pl.when(gets(up, j))
+            def _():
+                across(up, j).wait_recv()
+
+    wide = adj[...]
+
+    def back_of(block):
+        rows = [
+            kern[pl.ds(pl.multiple_of(index * CH + block * BLOCK, BLOCK), BLOCK), :] for index in range(9)
+        ]
+        return lax.dot_general(
+            jnp.concatenate(rows, axis=1), wide, (((1,), (1,)), ((), ())), preferred_element_type=F32
+        )
+
+    bk_c = []
+    for k in (2, 1, 3):
+        to_sect[k] = back_of(lax.rem(c + k, 4)).astype(BF16)
+        copy = remote(to_sect.at[k], from_sect.at[k], bk_s.at[k], bk_r.at[k], at_sect(k))
+        copy.start()
+        bk_c.append(copy)
+
+    conv_t = jnp.zeros((PIXELS, BLOCK), F32)
+    for col_step in (-1, 0, 1):
+        three = [OFFSETS.index((row_step, col_step)) * CH for row_step in (-1, 0, 1)]
+        value = jnp.dot(
+            mod_t[...],
+            jnp.concatenate([kern[row : row + CH, :] for row in three], axis=1),
+            preferred_element_type=F32,
+        )
+        by_row = value[:, BLOCK : 2 * BLOCK]
+        by_row = by_row + moved_rows(value[:, 0:BLOCK], -1, 0) + moved_rows(value[:, 2 * BLOCK :], 1, 0)
+        conv_t = conv_t + moved_rows(by_row, 0, col_step)
+    conv_out = jnp.transpose(conv_t)
+    demod_grad = jnp.sum(adjoint_f * conv_out, axis=1, keepdims=True)
+    egrad_all[0, 0] = as_row(-0.5 * demod_grad * demod * demod * demod)
+    eg_c = [
+        remote(egrad_all.at[0, 0], egrad_all.at[0, k], eg_s.at[k], eg_r.at[k], at_sample(k)) for k in (1, 2, 3)
+    ]
+    for copy in eg_c:
+        copy.start()
+    styled[0] = (conv_out * demod + column(bias[...])).astype(BF16)
     gz_c = []
     for k in (2, 1, 3):
         gy_c[k].wait_recv()
@@ -246,42 +330,6 @@
         copy.start()
         gz_c.append(copy)
 
-    for copy in w2_c:
-        copy.wait_recv()
-
-    wide = adj[...]
-
-    def back_of(block):
-        rows = [
-            kern[pl.ds(pl.multiple_of(index * CH + block * BLOCK, BLOCK), BLOCK), :] for index in range(9)
-        ]
-        return jnp.dot(jnp.concatenate(rows, axis=1), wide, preferred_element_type=F32)
-
-    bk_c = []
-    for k in (2, 1, 3):
-        to_sect[k] = back_of(lax.rem(c + k, 4)).astype(BF16)
-        copy = remote(to_sect.at[k], from_sect.at[k], bk_s.at[k], bk_r.at[k], at_sect(k))
-        copy.start()
-        bk_c.append(copy)
-
-    conv_out = jnp.zeros((BLOCK, PIXELS), F32)
-    for index in range(9):
-        row_step, col_step = OFFSETS[index]
-        value = lax.dot_general(
-            kern[index * CH : (index + 1) * CH, :],
-            mod[...],
-            (((0,), (0,)), ((), ())),
-            preferred_element_type=F32,
-        )
-        conv_out = conv_out + shifted_by(value, row_step, col_step)
-    demod_grad = jnp.sum(adjoint_f * conv_out, axis=1, keepdims=True)
-    egrad_all[0, 0] = as_row(-0.5 * demod_grad * demod * demod * demod)
-    eg_c = [
-        remote(egrad_all.at[0, 0], egrad_all.at[0, k], eg_s.at[k], eg_r.at[k], at_sample(k)) for k in (1, 2, 3)
-    ]
-    for copy in eg_c:
-        copy.start()
-    styled[0] = (conv_out * demod + column(bias[...])).astype(BF16)
     own_back = back_of(c)
     for copy in eg_c:
         copy.wait_recv()
@@ -304,7 +352,7 @@
     twice[0:CH] = coupling
     twice[CH : 2 * CH] = coupling
     first = pl.multiple_of((2 * s + d) * (HALF - CH), HALF - CH)
-    owned = weight[pl.ds(pl.multiple_of(d * HALF, HALF), HALF), :].astype(F32)
+    owned = kern[rows_of(s, d), :].astype(F32)
     grad_weight[...] = total + 2.0 * owned * twice[pl.ds(first, HALF), :]
 
     summed = own_back
@@ -313,13 +361,23 @@
         summed = summed + from_sect[k].astype(F32)
     grad_features[0] = (summed * style_col).astype(BF16)
 
-    for copy in style_c + mod_c + w_c + w2_c + en_c + gy_c + gz_c + bk_c + eg_c + [swap_style, swap_egrad]:
+    for copy in style_c + mod_c + en_c + gy_c + gz_c + bk_c + eg_c + [swap_style, swap_egrad]:
         copy.wait_send()
+    for j in range(3):
+        for up in (True, False):
+
+            @pl.when(sends(up, j))
+            def _():
+                along(up, j).wait_send()
+
+            @pl.when(gets(up, j))
+            def _():
+                across(up, j).wait_send()
 
 
 def fused(features, weight, style, bias, adjoint):
     vmem = pl.BlockSpec(memory_space=pltpu.VMEM)
-    dma = pltpu.SemaphoreType.DMA((4,))
+    dma = pltpu.SemaphoreType.DMA((6,))
     return tuple(
         pl.pallas_call(
             fused_kernel,
@@ -328,12 +386,17 @@
                 jax.ShapeDtypeStruct((HALF, BLOCK), F32),
                 jax.ShapeDtypeStruct(features.shape, BF16),
             ),
-            in_specs=[vmem] * 5,
+            in_specs=[pl.BlockSpec(memory_space=pltpu.HBM)] * 5,
             out_specs=(vmem,) * 3,
             scratch_shapes=[
+                pltpu.VMEM((BLOCK, PIXELS), BF16),
+                pltpu.VMEM((1, BLOCK), F32),
+                pltpu.VMEM((BLOCK, PIXELS), BF16),
+                pltpu.SemaphoreType.DMA((5,)),
                 pltpu.VMEM((9 * CH, BLOCK), BF16),
                 pltpu.VMEM((CH, PIXELS), BF16),
-                pltpu.VMEM((9 * BLOCK, PIXELS), BF16),
+                pltpu.VMEM((PIXELS, CH), BF16),
+                pltpu.VMEM((PIXELS, 9 * BLOCK), BF16),
                 pltpu.VMEM((9 * CH, BLOCK), F32),
                 pltpu.VMEM((9 * CH, BLOCK), BF16),
                 pltpu.VMEM((4, HALF, BLOCK), BF16),
@@ -349,7 +412,7 @@
             ]
             + [dma] * 20,
             compiler_params=pltpu.CompilerParams(
-                collective_id=0, has_side_effects=True, vmem_limit_bytes=40 * 1024 * 1024
+                collective_id=0, has_side_effects=True, vmem_limit_bytes=64 * 1024 * 1024
             ),
         )(features, weight, style, bias.reshape(1, BLOCK), adjoint)
     )

time: 61.3 us -> 53.4 us (0.87)
  Pallas kernels: 54.3 us -> 48.6 us
  local copies, waits for them, and re-layouts: 6.12 us -> 3.96 us
    pallas_call x1, Pallas kernels: 54.3 us -> 48.6 us  [fused(): pl.pallas_call(fused_kernel, out_shape=(jax.ShapeDtypeStruct(features.sha...]
    unnamed x13 -> x5, local copies, waits for them, and re-layouts: 6.12 us -> 3.96 us
where the time goes in v2:
time: 53.4 us; the launch traced here: 53.2 us
  Pallas kernels  48.6 us (91%)
  local copies, waits for them, and re-layouts  3.96 us (7%)
  between operations  0.64 us (1%)
    pallas_call x1, Pallas kernels, fused(): pl.pallas_call(fused_kernel, out_shape=(jax.ShapeDtypeStruct(features.sha...  48.6 us
    unnamed x5, local copies, waits for them, and re-layouts  3.96 us

profile of v2, /device:TPU:0, one launch (start us, length us, event | category | flops | bytes accessed | tf_op | source)
XLA Modules:
  0.0 53.2 jit_solution(9553102192351175026)
XLA Ops:
  0.6 48.6 %shard_map.76 = (bf16[1,128,512]{2,1,0:T(8,128)(2,1)}, f32[576,128]{1,0:T(8,128)}, bf16[1,128,512]{2,1,0:T(8,128)(2,1)}) custom-call(bf16[1,128,512]{2,1,0:T(8,128)(2,1)} %features_h.1, bf16[1152,128]{1,0:T(8,128)(2,1)} %weight_h.1, f32[1,512]{1,0:T(1,128)} %style_h.1, f32[1,128]{1,0:T(1,128)} %bitcast.1, bf16[1,128,512]{2,1,0:T(8,128)(2,1)} %adjoint_h.1), custom_call_target="tpu_custom_call" | custom-call | tf_op jit(solution)/shard_map/pallas_call | solution.py:382
  49.3 1.6 %copy.11 = bf16[1,128,512]{2,1,0:T(8,128)(2,1)} copy(bf16[1,128,512]{2,1,0:T(8,128)(2,1)} %get-tuple-element.6) | data formatting | bytes 262144
  50.9 0.0 copy-start
  50.9 1.7 %copy.12 = f32[576,128]{1,0:T(8,128)} copy(f32[576,128]{1,0:T(8,128)} %get-tuple-element.7) | data formatting | bytes 589824
  52.6 0.0 copy-done
  52.6 0.7 %copy.13 = bf16[1,128,512]{2,1,0:T(8,128)(2,1)} copy(bf16[1,128,512]{2,1,0:T(8,128)(2,1)S(1)} %copy-done) | data formatting | bytes 262144
Async XLA Ops:
  50.9 1.7 %copy-start = (bf16[1,128,512]{2,1,0:T(8,128)(2,1)S(1)}, bf16[1,128,512]{2,1,0:T(8,128)(2,1)}, u32[]{:S(2)}) copy-start(bf16[1,128,512]{2,1,0:T(8,128)(2,1)} %get-tuple-element.8) | copy-start | bytes 393220

commit v3 on v2

--- a/solution.py
+++ b/solution.py
@@ -105,16 +105,12 @@
     return jnp.transpose(jnp.broadcast_to(row, (BLOCK, BLOCK)))[:, 0:1]
 
 
-def as_row(col):
-    return jnp.transpose(jnp.broadcast_to(col, (BLOCK, BLOCK)))[0:1, :]
-
-
 def fused_kernel(
     features_h, weight_h, style_h, bias_h, adjoint_h, styled, grad_weight, grad_features,
-    features, bias, adjoint, in_s, kern, mod, mod_t, adj, grad, grad_b, from_dom, to_sample, from_sample, to_sect, from_sect,
+    features, bias, adjoint, in_s, kern, mod, mod_t, adj, adj_t, grad, given, from_dom, to_sample, from_sample, to_sect, from_sect,
     twice, style_all, energy_out, energy_in, egrad_all,
     style_s, style_r, mod_s, mod_r, w_s, w_r, w2_s, w2_r, en_s, en_r,
-    gy_s, gy_r, gz_s, gz_r, bk_s, bk_r, eg_s, eg_r, swap_s, swap_r,
+    gy_s, gy_r, gz_s, gz_r, bk_s, bk_r, eg_s, eg_r,
 ):
     s = lax.axis_index("sample")
     c = lax.axis_index("sect")
@@ -126,6 +122,9 @@
 
     def at_sect(k):
         return {"sect": lax.rem(c + k, 4)}
+
+    def at_cross(k):
+        return {"sample": lax.rem(s + k, 4), "dom": other}
 
     partner = {"dom": other}
 
@@ -153,16 +152,11 @@
 
     barrier = pltpu.get_barrier_semaphore()
     for k in (1, 2, 3):
-        pl.semaphore_signal(barrier, inc=1, device_id=at_sample(k), device_id_type=MESH)
-        pl.semaphore_signal(barrier, inc=1, device_id=at_sect(k), device_id_type=MESH)
+        for where in (at_sample(k), at_cross(k), at_sect(k)):
+            pl.semaphore_signal(barrier, inc=1, device_id=where, device_id_type=MESH)
     pl.semaphore_signal(barrier, inc=1, device_id=partner, device_id_type=MESH)
 
     own_channels = pl.ds(pl.multiple_of(c * BLOCK, BLOCK), BLOCK)
-    for load in loads[0:3]:
-        load.wait()
-    style_col = column(style_all[0, 0, :, own_channels])
-    mod[own_channels, :] = (features[...].astype(F32) * style_col).astype(BF16)
-
     def rows_of(shard, part):
         return pl.ds(pl.multiple_of(shard * OWN + part * HALF, HALF), HALF)
 
@@ -196,6 +190,35 @@
                 def _():
                     along(up, j + 1).start()
 
+    def to_others(array, send, recv):
+        peers = [(0, k, at_sample(k)) for k in (1, 2, 3)] + [(1, k, at_cross(k)) for k in range(4)]
+        copies = [
+            remote(array.at[0, 0], array.at[h, k], send.at[h, k], recv.at[h, k], where) for h, k, where in peers
+        ]
+        for copy in copies:
+            copy.start()
+        return copies
+
+    loads[0].wait()
+    loads[2].wait()
+    pl.semaphore_wait(barrier, 10)
+
+    style_c = to_others(style_all, style_s, style_r)
+    for up in (True, False):
+
+        @pl.when(sends(up, 0))
+        def _():
+            along(up, 0).start()
+
+    loads[1].wait()
+    style_col = column(style_all[0, 0, :, own_channels])
+    mod[own_channels, :] = (features[...].astype(F32) * style_col).astype(BF16)
+
+    mod_c = [
+        remote(mod.at[own_channels], mod.at[own_channels], mod_s.at[k], mod_r.at[k], at_sect(k)) for k in (1, 2, 3)
+    ]
+    for copy in mod_c:
+        copy.start()
     squares = kern[own_rows, :].astype(F32)
     squares = squares * squares
     part = squares[0:CH] + squares[CH : 2 * CH]
@@ -206,28 +229,8 @@
     twice[CH + BLOCK : 2 * CH] = part[BLOCK:]
     kernel_sq = twice[pl.ds(pl.multiple_of(CH - s * BLOCK, BLOCK), CH), :]
 
-    pl.semaphore_wait(barrier, 7)
-
-    style_c = [
-        remote(style_all.at[0, 0], style_all.at[0, k], style_s.at[k], style_r.at[k], at_sample(k)) for k in (1, 2, 3)
-    ]
-    for copy in style_c:
-        copy.start()
-    for up in (True, False):
-
-        @pl.when(sends(up, 0))
-        def _():
-            along(up, 0).start()
-
-    mod_c = [
-        remote(mod.at[own_channels], mod.at[own_channels], mod_s.at[k], mod_r.at[k], at_sect(k)) for k in (1, 2, 3)
-    ]
-    for copy in mod_c:
-        copy.start()
-    for copy in style_c:
+    for copy in style_c[0:3]:
         copy.wait_recv()
-    swap_style = remote(style_all.at[0], style_all.at[1], swap_s.at[0], swap_r.at[0], partner)
-    swap_style.start()
     styles = jnp.concatenate([style_all[0, k] for k in range(4)] * 2, axis=0)
     terms = jnp.dot(styles * styles, kernel_sq, precision=HIGH, preferred_element_type=F32)
     for k in range(4):
@@ -238,19 +241,12 @@
     for copy in en_c:
         copy.start()
     pass_on(0)
-    energy = energy_out[0] + EPSILON
-    for k in (1, 2, 3):
-        en_c[k - 1].wait_recv()
-        energy = energy + energy_in[k]
-    demod = column(lax.rsqrt(energy))
 
     loads[3].wait()
     loads[4].wait()
-    adjoint_f = adjoint[...].astype(F32)
-    scaled = (adjoint_f * demod).astype(BF16).astype(F32)
-    scaled_t = jnp.transpose(scaled)
+    adj_t[...] = jnp.transpose(adjoint[...].astype(F32))
     for col_step in (-1, 0, 1):
-        by_col = moved_rows(scaled_t, 0, -col_step)
+        by_col = moved_rows(adj_t[...], 0, -col_step)
         for row_step in (-1, 0, 1):
             index = OFFSETS.index((row_step, col_step))
             adj[:, index * BLOCK : (index + 1) * BLOCK] = moved_rows(by_col, -row_step, 0).astype(BF16)
@@ -262,21 +258,38 @@
         last = min(index + 2, 9)
         value = jnp.dot(mod[...], adj[:, index * BLOCK : last * BLOCK], preferred_element_type=F32)
         for one in range(index, last):
-            block = value[:, (one - index) * BLOCK : (one - index + 1) * BLOCK]
-            grad[one * CH : (one + 1) * CH, :] = block
-            grad_b[one * CH : (one + 1) * CH, :] = block.astype(BF16)
-    gy_c = [
-        remote(
-            grad_b.at[rows_of(lax.rem(s + k, 4), other)], from_dom.at[k], gy_s.at[k], gy_r.at[k], partner
-        )
-        for k in range(4)
-    ]
-    order = (2, 1, 3, 0)
-    for k in order:
-        gy_c[k].start()
-
+            grad[one * CH : (one + 1) * CH, :] = value[:, (one - index) * BLOCK : (one - index + 1) * BLOCK]
+    energy = energy_out[0] + EPSILON
+    for k in (1, 2, 3):
+        en_c[k - 1].wait_recv()
+        energy = energy + energy_in[k]
+    demod = lax.rsqrt(energy)
+
+    def kept(k):
+        return grad[rows_of(lax.rem(s + k, 4), d), :] * demod
+
+    def give(k):
+        given[k] = (grad[rows_of(lax.rem(s + k, 4), other), :] * demod).astype(BF16)
+        copy = remote(given.at[k], from_dom.at[k], gy_s.at[k], gy_r.at[k], partner)
+        copy.start()
+        return copy
+
+    def hand_on(k):
+        gy_c[k].wait_recv()
+        to_sample[k] = (kept(k) + from_dom[k].astype(F32)).astype(BF16)
+        copy = remote(to_sample.at[k], from_sample.at[k], gz_s.at[k], gz_r.at[k], at_sample(k))
+        copy.start()
+        return copy
+
+    gy_c = {2: give(2), 1: give(1)}
     pass_on(2)
+    gy_c[3] = give(3)
+    gy_c[0] = give(0)
     mod_t[...] = jnp.transpose(mod[...])
+    for index in range(9):
+        part = slice(index * BLOCK, (index + 1) * BLOCK)
+        adj[:, part] = (adj[:, part].astype(F32) * demod).astype(BF16)
+    gz_c = [hand_on(2), hand_on(1)]
     for j in range(3):
         for up in (True, False):
 
@@ -301,6 +314,7 @@
         copy.start()
         bk_c.append(copy)
 
+    gz_c.append(hand_on(3))
     conv_t = jnp.zeros((PIXELS, BLOCK), F32)
     for col_step in (-1, 0, 1):
         three = [OFFSETS.index((row_step, col_step)) * CH for row_step in (-1, 0, 1)]
@@ -312,38 +326,19 @@
         by_row = value[:, BLOCK : 2 * BLOCK]
         by_row = by_row + moved_rows(value[:, 0:BLOCK], -1, 0) + moved_rows(value[:, 2 * BLOCK :], 1, 0)
         conv_t = conv_t + moved_rows(by_row, 0, col_step)
-    conv_out = jnp.transpose(conv_t)
-    demod_grad = jnp.sum(adjoint_f * conv_out, axis=1, keepdims=True)
-    egrad_all[0, 0] = as_row(-0.5 * demod_grad * demod * demod * demod)
-    eg_c = [
-        remote(egrad_all.at[0, 0], egrad_all.at[0, k], eg_s.at[k], eg_r.at[k], at_sample(k)) for k in (1, 2, 3)
-    ]
-    for copy in eg_c:
-        copy.start()
-    styled[0] = (conv_out * demod + column(bias[...])).astype(BF16)
-    gz_c = []
-    for k in (2, 1, 3):
-        gy_c[k].wait_recv()
-        kept = grad[rows_of(lax.rem(s + k, 4), d), :]
-        to_sample[k] = (kept + from_dom[k].astype(F32)).astype(BF16)
-        copy = remote(to_sample.at[k], from_sample.at[k], gz_s.at[k], gz_r.at[k], at_sample(k))
-        copy.start()
-        gz_c.append(copy)
-
+    demod_grad = jnp.sum(adj_t[...] * conv_t, axis=0, keepdims=True)
+    egrad_all[0, 0] = -0.5 * demod_grad * demod * demod * demod
+    eg_c = to_others(egrad_all, eg_s, eg_r)
+    styled[0] = jnp.transpose(conv_t * demod + bias[...]).astype(BF16)
     own_back = back_of(c)
-    for copy in eg_c:
-        copy.wait_recv()
-    swap_egrad = remote(egrad_all.at[0], egrad_all.at[1], swap_s.at[1], swap_r.at[1], partner)
-    swap_egrad.start()
-
     gy_c[0].wait_recv()
-    total = grad[rows_of(s, d), :] + from_dom[0].astype(F32)
+    total = kept(0) + from_dom[0].astype(F32)
     for k, copy in zip((2, 1, 3), gz_c):
         copy.wait_recv()
         total = total + from_sample[k].astype(F32)
 
-    swap_style.wait_recv()
-    swap_egrad.wait_recv()
+    for copy in style_c[3:] + eg_c:
+        copy.wait_recv()
     styles = jnp.concatenate([style_all[h, k] for h in range(2) for k in range(4)], axis=0)
     egrads = jnp.concatenate([egrad_all[h, k] for h in range(2) for k in range(4)], axis=0)
     coupling = lax.dot_general(
@@ -361,7 +356,7 @@
         summed = summed + from_sect[k].astype(F32)
     grad_features[0] = (summed * style_col).astype(BF16)
 
-    for copy in style_c + mod_c + en_c + gy_c + gz_c + bk_c + eg_c + [swap_style, swap_egrad]:
+    for copy in style_c + mod_c + en_c + list(gy_c.values()) + gz_c + bk_c + eg_c:
         copy.wait_send()
     for j in range(3):
         for up in (True, False):
@@ -378,13 +373,14 @@
 def fused(features, weight, style, bias, adjoint):
     vmem = pl.BlockSpec(memory_space=pltpu.VMEM)
     dma = pltpu.SemaphoreType.DMA((6,))
+    by_dom = pltpu.SemaphoreType.DMA((2, 4))
     return tuple(
         pl.pallas_call(
             fused_kernel,
             out_shape=(
-                jax.ShapeDtypeStruct(features.shape, BF16),
-                jax.ShapeDtypeStruct((HALF, BLOCK), F32),
-                jax.ShapeDtypeStruct(features.shape, BF16),
+                pltpu.VMEM(features.shape, BF16),
+                pltpu.VMEM((HALF, BLOCK), F32),
+                pltpu.VMEM(features.shape, BF16),
             ),
             in_specs=[pl.BlockSpec(memory_space=pltpu.HBM)] * 5,
             out_specs=(vmem,) * 3,
@@ -397,8 +393,9 @@
                 pltpu.VMEM((CH, PIXELS), BF16),
                 pltpu.VMEM((PIXELS, CH), BF16),
                 pltpu.VMEM((PIXELS, 9 * BLOCK), BF16),
+                pltpu.VMEM((PIXELS, BLOCK), F32),
                 pltpu.VMEM((9 * CH, BLOCK), F32),
-                pltpu.VMEM((9 * CH, BLOCK), BF16),
+                pltpu.VMEM((4, HALF, BLOCK), BF16),
                 pltpu.VMEM((4, HALF, BLOCK), BF16),
                 pltpu.VMEM((4, HALF, BLOCK), BF16),
                 pltpu.VMEM((4, HALF, BLOCK), BF16),
@@ -410,9 +407,9 @@
                 pltpu.VMEM((4, 1, BLOCK), F32),
                 pltpu.VMEM((2, 4, 1, BLOCK), F32),
             ]
-            + [dma] * 20,
+            + [by_dom] * 2 + [dma] * 14 + [by_dom] * 2,
             compiler_params=pltpu.CompilerParams(
-                collective_id=0, has_side_effects=True, vmem_limit_bytes=64 * 1024 * 1024
+                collective_id=0, has_side_effects=True, vmem_limit_bytes=66478080
             ),
         )(features, weight, style, bias.reshape(1, BLOCK), adjoint)
     )

time: 53.4 us -> 43.2 us (0.81)
  Pallas kernels: 48.6 us -> 40.3 us
  local copies, waits for them, and re-layouts: 3.96 us -> 2.03 us
    pallas_call x1, Pallas kernels: 48.6 us -> 40.3 us  [fused(): pl.pallas_call(fused_kernel, out_shape=(pltpu.VMEM(features.shape, BF16),...]
    unnamed x5 -> x3, local copies, waits for them, and re-layouts: 3.96 us -> 2.03 us
where the time goes in v3:
time: 43.2 us; the launch traced here: 43 us
  Pallas kernels  40.3 us (93%)
  local copies, waits for them, and re-layouts  2.03 us (5%)
  between operations  0.64 us (1%)
    pallas_call x1, Pallas kernels, fused(): pl.pallas_call(fused_kernel, out_shape=(pltpu.VMEM(features.shape, BF16),...  40.3 us
    unnamed x3, local copies, waits for them, and re-layouts  2.03 us

profile of v3, /device:TPU:0, one launch (start us, length us, event | category | flops | bytes accessed | tf_op | source)
XLA Modules:
  0.0 43.0 jit_solution(5305642178328813044)
XLA Ops:
  0.6 40.3 %shard_map.76 = (bf16[1,128,512]{2,1,0:T(8,128)(2,1)S(1)}, f32[576,128]{1,0:T(8,128)S(1)}, bf16[1,128,512]{2,1,0:T(8,128)(2,1)S(1)}) custom-call(bf16[1,128,512]{2,1,0:T(8,128)(2,1)} %features_h.1, bf16[1152,128]{1,0:T(8,128)(2,1)} %weight_h.1, f32[1,512]{1,0:T(1,128)} %style_h.1, f32[1,128]{1,0:T(1,128)} %bitcast.1, bf16[1,128,512]{2,1,0:T(8,128)(2,1)} %adjoint_h.1), custom_call_target="tpu_custom_call" | custom-call | tf_op jit(solution)/shard_map/pallas_call | solution.py:378
  41.0 0.7 %copy.11 = bf16[1,128,512]{2,1,0:T(8,128)(2,1)} copy(bf16[1,128,512]{2,1,0:T(8,128)(2,1)S(1)} %get-tuple-element.3) | data formatting | bytes 262144
  41.6 0.7 %copy.13 = bf16[1,128,512]{2,1,0:T(8,128)(2,1)} copy(bf16[1,128,512]{2,1,0:T(8,128)(2,1)S(1)} %get-tuple-element.5) | data formatting | bytes 262144
  42.3 0.7 %copy.12 = f32[576,128]{1,0:T(8,128)} copy(f32[576,128]{1,0:T(8,128)S(1)} %get-tuple-element.4) | data formatting | bytes 589824

commit v4 on v3

--- a/solution.py
+++ b/solution.py
@@ -182,13 +182,16 @@
             @pl.when(gets(up, j))
             def _():
                 along(up, j).wait_recv()
-                across(up, j).start()
 
             if j < 2:
 
                 @pl.when(sends(up, j + 1))
                 def _():
                     along(up, j + 1).start()
+
+            @pl.when(gets(up, j))
+            def _():
+                across(up, j).start()
 
     def to_others(array, send, recv):
         peers = [(0, k, at_sample(k)) for k in (1, 2, 3)] + [(1, k, at_cross(k)) for k in range(4)]
@@ -331,12 +334,6 @@
     eg_c = to_others(egrad_all, eg_s, eg_r)
     styled[0] = jnp.transpose(conv_t * demod + bias[...]).astype(BF16)
     own_back = back_of(c)
-    gy_c[0].wait_recv()
-    total = kept(0) + from_dom[0].astype(F32)
-    for k, copy in zip((2, 1, 3), gz_c):
-        copy.wait_recv()
-        total = total + from_sample[k].astype(F32)
-
     for copy in style_c[3:] + eg_c:
         copy.wait_recv()
     styles = jnp.concatenate([style_all[h, k] for h in range(2) for k in range(4)], axis=0)
@@ -348,13 +345,19 @@
     twice[CH : 2 * CH] = coupling
     first = pl.multiple_of((2 * s + d) * (HALF - CH), HALF - CH)
     owned = kern[rows_of(s, d), :].astype(F32)
-    grad_weight[...] = total + 2.0 * owned * twice[pl.ds(first, HALF), :]
-
     summed = own_back
     for k, copy in zip((2, 1, 3), bk_c):
         copy.wait_recv()
         summed = summed + from_sect[k].astype(F32)
     grad_features[0] = (summed * style_col).astype(BF16)
+
+    gy_c[0].wait_recv()
+    total = kept(0) + from_dom[0].astype(F32)
+    for k, copy in zip((2, 1, 3), gz_c):
+        copy.wait_recv()
+        total = total + from_sample[k].astype(F32)
+
+    grad_weight[...] = total + 2.0 * owned * twice[pl.ds(first, HALF), :]
 
     for copy in style_c + mod_c + en_c + list(gy_c.values()) + gz_c + bk_c + eg_c:
         copy.wait_send()

time: 43.2 us -> 43.3 us (level)
  no operation moved by 1% of the time
where the time goes in v4:
time: 43.3 us; the launch traced here: 43.2 us
  Pallas kernels  40.5 us (94%)
  local copies, waits for them, and re-layouts  2.03 us (5%)
  between operations  0.64 us (1%)
    pallas_call x1, Pallas kernels, fused(): pl.pallas_call(fused_kernel, out_shape=(pltpu.VMEM(features.shape, BF16),...  40.5 us
    unnamed x3, local copies, waits for them, and re-layouts  2.03 us

profile of v4, /device:TPU:0, one launch (start us, length us, event | category | flops | bytes accessed | tf_op | source)
XLA Modules:
  0.0 43.2 jit_solution(2444581463007609510)
XLA Ops:
  0.6 40.5 %shard_map.76 = (bf16[1,128,512]{2,1,0:T(8,128)(2,1)S(1)}, f32[576,128]{1,0:T(8,128)S(1)}, bf16[1,128,512]{2,1,0:T(8,128)(2,1)S(1)}) custom-call(bf16[1,128,512]{2,1,0:T(8,128)(2,1)} %features_h.1, bf16[1152,128]{1,0:T(8,128)(2,1)} %weight_h.1, f32[1,512]{1,0:T(1,128)} %style_h.1, f32[1,128]{1,0:T(1,128)} %bitcast.1, bf16[1,128,512]{2,1,0:T(8,128)(2,1)} %adjoint_h.1), custom_call_target="tpu_custom_call" | custom-call | tf_op jit(solution)/shard_map/pallas_call | solution.py:381
  41.1 0.7 %copy.11 = bf16[1,128,512]{2,1,0:T(8,128)(2,1)} copy(bf16[1,128,512]{2,1,0:T(8,128)(2,1)S(1)} %get-tuple-element.3) | data formatting | bytes 262144
  41.8 0.7 %copy.13 = bf16[1,128,512]{2,1,0:T(8,128)(2,1)} copy(bf16[1,128,512]{2,1,0:T(8,128)(2,1)S(1)} %get-tuple-element.5) | data formatting | bytes 262144
  42.5 0.7 %copy.12 = f32[576,128]{1,0:T(8,128)} copy(f32[576,128]{1,0:T(8,128)S(1)} %get-tuple-element.4) | data formatting | bytes 589824
